TPU v7x, 256 devices: a whole 4x4x8 slice. The times are simulated.
256 devices in a mesh: dp: 32 (over x, z_lo, y), space: 8 (over z_hi, core).
Axes of the slice: x: 4, y: 4, z: 8 (z_hi: 4, z_lo: 2; z = z_hi * 2 + z_lo), core: 2. Of those that a mesh axis runs over, the one named last changes fastest.
Arguments:
- members: bfloat16 [32, 48, 100, 768], P('dp', 'space'), may hold values from -6 to 6
- cotangent: bfloat16 [32, 48, 100, 768], P('dp', 'space'), may hold values from -6 to 6
- gain: float32 [768], replicated, may hold values from 0.5 to 1.5
- weight_one: float32 [8, 2, 96, 96], replicated, may hold values from -0.4375 to 0.4375
- bias_one: float32 [8, 2, 96], replicated, may hold values from -3 to 3
- weight_two: float32 [8, 2, 96, 96], replicated, may hold values from -0.4375 to 0.4375
- bias_two: float32 [8, 2, 96], replicated, may hold values from -0.3 to 0.3
Outputs:
- mixed: bfloat16 [32, 48, 100, 768], P('dp', 'space')
- grad_weight_one: float32 [8, 2, 96, 96], P('space')
- grad_bias_one: float32 [8, 2, 96], P('space')
- grad_weight_two: float32 [8, 2, 96, 96], P('space')
- grad_bias_two: float32 [8, 2, 96], P('space')
All inputs are finite; a program needn't handle non-finite values.
Results may differ from a plain program's by a relative error of at most 0.015.
Values sent between devices are 32-bit elements; how exact they have to be, the bound alone decides.
A program may use at most 128 MiB of HBM per device.

v0:
```python
import math

import jax
import jax.numpy as jnp
from jax import lax
from jax.sharding import PartitionSpec as P

KW = 48


shrink = 0.01


def contract(form, left, right):
    return jnp.einsum(form, left, right, precision=lax.Precision.HIGHEST)


def lon_tables(width, kept):
    columns = jnp.arange(width, dtype=jnp.int32)
    wavenums = jnp.arange(kept, dtype=jnp.int32)
    phase = (wavenums[:, None] * columns[None, :] % width).astype(jnp.float32) * (
        2.0 * math.pi / width
    )
    scale = 1.0 / math.sqrt(width)
    return (jnp.cos(phase) * scale, -jnp.sin(phase) * scale)


def lat_tables(length):
    rows = jnp.arange(length, dtype=jnp.int32)
    phase = (rows[:, None] * rows[None, :] % length).astype(jnp.float32) * (2.0 * math.pi / length)
    scale = 1.0 / math.sqrt(length)
    return (jnp.cos(phase) * scale, -jnp.sin(phase) * scale)


def mode_weights(kept):
    wavenums = jnp.arange(kept, dtype=jnp.int32)
    return jnp.where(wavenums == 0, 1.0, 2.0).astype(jnp.float32)


def layer_norm(values, gain):
    center = values - jnp.mean(values, axis=-1, keepdims=True)
    spread = jnp.mean(center * center, axis=-1, keepdims=True)
    return center * lax.rsqrt(spread + 1e-05) * gain


def lat_forward(real_part, imag_part, lat_cos, lat_sin):
    out_real = contract("mh,hkc->mkc", lat_cos, real_part) - contract(
        "mh,hkc->mkc", lat_sin, imag_part
    )
    out_imag = contract("mh,hkc->mkc", lat_cos, imag_part) + contract(
        "mh,hkc->mkc", lat_sin, real_part
    )
    return (out_real, out_imag)


def lat_inverse(real_part, imag_part, lat_cos, lat_sin):
    out_real = contract("mh,mkc->hkc", lat_cos, real_part) + contract(
        "mh,mkc->hkc", lat_sin, imag_part
    )
    out_imag = contract("mh,mkc->hkc", lat_cos, imag_part) - contract(
        "mh,mkc->hkc", lat_sin, real_part
    )
    return (out_real, out_imag)


def filter_modes(real_part, imag_part, weight_one, bias_one, weight_two, bias_two):
    blocks = weight_one.shape[0]
    width = weight_one.shape[2]
    shape = real_part.shape
    inp_real = real_part.reshape(shape[:-1] + (blocks, width))
    inp_imag = imag_part.reshape(shape[:-1] + (blocks, width))
    form = "...bi,bio->...bo"
    first_real = jax.nn.relu(
        contract(form, inp_real, weight_one[:, 0])
        - contract(form, inp_imag, weight_one[:, 1])
        + bias_one[:, 0]
    )
    first_imag = jax.nn.relu(
        contract(form, inp_imag, weight_one[:, 0])
        + contract(form, inp_real, weight_one[:, 1])
        + bias_one[:, 1]
    )
    second_real = (
        contract(form, first_real, weight_two[:, 0])
        - contract(form, first_imag, weight_two[:, 1])
        + bias_two[:, 0]
    )
    second_imag = (
        contract(form, first_imag, weight_two[:, 0])
        + contract(form, first_real, weight_two[:, 1])
        + bias_two[:, 1]
    )
    second_real = second_real - jnp.clip(second_real, -shrink, shrink)
    second_imag = second_imag - jnp.clip(second_imag, -shrink, shrink)
    return (second_real.reshape(shape), second_imag.reshape(shape))


def shards(members, cotangent, gain, weight_one, bias_one, weight_two, bias_two):
    groups = lax.axis_size("space")
    member_count = members.shape[0]
    lat_rows = members.shape[1] * groups
    width = members.shape[2]
    lon_cos, lon_sin = lon_tables(width, KW)
    lat_cos, lat_sin = lat_tables(lat_rows)
    factor = mode_weights(KW)[:, None]
    params = (weight_one, bias_one, weight_two, bias_two)
    field = members[0].astype(jnp.float32)
    normed = layer_norm(field, gain)
    spec = jnp.stack(
        [contract("kw,hwc->hkc", lon_cos, normed), contract("kw,hwc->hkc", lon_sin, normed)], 1
    )
    cot = cotangent[0].astype(jnp.float32)
    cspec = jnp.stack(
        [
            contract("kw,hwc->hkc", lon_cos * factor, cot),
            contract("kw,hwc->hkc", lon_sin * factor, cot),
        ],
        1,
    )
    spec_got = lax.all_to_all(spec, "space", split_axis=2, concat_axis=0, tiled=True)
    cspec_got = lax.all_to_all(cspec, "space", split_axis=2, concat_axis=0, tiled=True)
    spec_real, spec_imag = lat_forward(spec_got[:, 0], spec_got[:, 1], lat_cos, lat_sin)

    def apply(first_w, first_b, second_w, second_b):
        return filter_modes(spec_real, spec_imag, first_w, first_b, second_w, second_b)

    (filt_real, filt_imag), pullback = jax.vjp(apply, *params)
    back_real, back_imag = lat_inverse(filt_real, filt_imag, lat_cos, lat_sin)
    stacked = jnp.stack([back_real, back_imag], 1)
    returned = lax.all_to_all(stacked, "space", split_axis=0, concat_axis=2, tiled=True)
    spectral = contract("kw,hkc->hwc", lon_cos * factor, returned[:, 0]) + contract(
        "kw,hkc->hwc", lon_sin * factor, returned[:, 1]
    )
    outputs = [(field + normed + spectral).astype(jnp.bfloat16)]
    dspec_real, dspec_imag = lat_forward(cspec_got[:, 0], cspec_got[:, 1], lat_cos, lat_sin)
    grads = pullback((dspec_real, dspec_imag))
    shares = (
        lax.psum_scatter(grads[0], "space", scatter_dimension=0, tiled=True),
        lax.psum_scatter(grads[1], "space", scatter_dimension=0, tiled=True),
        lax.psum_scatter(grads[2], "space", scatter_dimension=0, tiled=True),
        lax.psum_scatter(grads[3], "space", scatter_dimension=0, tiled=True),
    )
    summed = lax.psum((shares[0], shares[1], shares[2], shares[3]), "dp")
    norm = 1.0 / math.sqrt(lax.axis_size("dp") * member_count * lat_rows * KW)
    return (
        jnp.stack(outputs, 0),
        summed[0] * norm,
        summed[1] * norm,
        summed[2] * norm,
        summed[3] * norm,
    )


def solution(mesh):
    in_specs = (P("dp", "space", None, None), P("dp", "space", None, None), P(), P(), P(), P(), P())
    out_specs = (
        P("dp", "space", None, None),
        P("space", None, None, None),
        P("space", None, None),
        P("space", None, None, None),
        P("space", None, None),
    )
    return jax.shard_map(shards, mesh=mesh, in_specs=in_specs, out_specs=out_specs, check_vma=False)
```

profile of v0, /device:TPU:32, one launch (start us, length us, event | category | flops | bytes accessed | tf_op | source)
XLA Modules:
  0.0 658.2 jit_solution(10956104711450330161)
XLA Ops:
  9.8 2.6 copy.131
  12.4 7.7 %all-to-all-start.2 = ((f32[6,2,48,768]{3,1,0,2:T(2,128)}), f32[6,2,48,768]{3,1,0,2:T(2,128)S(1)}, u32[]{:S(2)}, u32[]{:S(2)}) async-start(f32[6,2,48,768]{3,1,0,2:T(2,128)} %copy.131), calls=%async_computation.2 | async-start | bytes 3538944 | tf_op jit(solution)/shard_map/all_to_all | solution.py:121
  20.8 1.7 fusion.21
  22.5 1.7 fusion.24
  24.4 2.6 copy.108
  27.0 37.8 %all-to-all-done.2 = f32[6,2,48,768]{3,1,0,2:T(2,128)S(1)} async-done(((f32[6,2,48,768]{3,1,0,2:T(2,128)}), f32[6,2,48,768]{3,1,0,2:T(2,128)S(1)}, u32[]{:S(2)}, u32[]{:S(2)}) %all-to-all-start.2) | async-done | bytes 1769504 | tf_op jit(solution)/shard_map/all_to_all | solution.py:121
  64.8 4.5 all-to-all-start
  72.9 1.9 convolution_add_fusion.4
  74.8 2.8 reshape.71
  77.5 1.9 fusion.88
  79.4 34.4 %all-to-all-done = f32[6,2,48,768]{3,1,0,2:T(2,128)} async-done(((f32[6,2,48,768]{3,1,0,2:T(2,128)}), f32[6,2,48,768]{3,1,0,2:T(2,128)}, u32[]{:S(2)}, u32[]{:S(2)}) %all-to-all-start) | async-done | bytes 1769504 | tf_op jit(solution)/shard_map/all_to_all | solution.py:120
  113.9 2.1 copy.110
  118.3 1.9 fusion.85
  120.3 1.9 convolution_add_fusion.6
  122.1 1.7 reshape.68
  123.8 3.3 convolution_subtract_fusion.4
  127.1 1.7 reshape.67
  128.8 3.3 fusion.60
  132.2 2.3 fusion.66
  134.5 1.9 convolution_subtract_fusion.2
  136.4 2.8 reshape.72
  139.2 2.6 fusion.121
  146.9 3.0 fusion.312
  151.6 3.6 fusion.314
  156.6 3.3 convolution_bitcast_fusion.6
  159.9 3.3 convolution_bitcast_fusion.7
  164.7 1.6 fusion.322
  166.3 3.3 convolution_bitcast_fusion.8
  169.7 3.3 convolution_bitcast_fusion.9
  173.0 3.2 convolution_bitcast_fusion.2
  177.3 1.9 fusion.139
  179.2 1.7 copy.121
  180.9 1.6 reshape.69
  186.1 2.6 copy.127
  188.6 4.4 all-to-all-start.1
  193.2 2.1 pad_add_fusion.1
  195.2 2.5 convolution_bitcast_fusion.3
  197.7 2.5 convolution_bitcast_fusion.4
  200.2 2.5 convolution_bitcast_fusion.5
  205.0 55.7 %all-reduce.18 = (f32[8,2,96]{2,1,0:T(2,128)S(1)}, f32[8,2,96]{2,1,0:T(2,128)S(1)}) all-reduce(f32[8,2,96]{2,1,0:T(2,128)S(1)} %pad_add_fusion.3, f32[8,2,96]{2,1,0:T(2,128)S(1)} %pad_add_fusion.2), channel_id=3, replica_groups=mesh['dp'=32,'space'=8] {'space'}, use_global_device_ids=true, to_apply=%region_6.8.clone | all-reduce | flops 3072 | bytes 24576
  261.4 75.4 %all-reduce.16 = (f32[1,2,96]{2,1,0:T(2,128)S(1)}, f32[1,2,96]{2,1,0:T(2,128)S(1)}) all-reduce(f32[1,2,96]{2,1,0:T(2,128)S(1)} %get-tuple-element.72, f32[1,2,96]{2,1,0:T(2,128)S(1)} %get-tuple-element.71), channel_id=1, replica_groups=mesh['dp'=32,'space'=8] {'dp'}, use_global_device_ids=true, to_apply=%region_7.9 | all-reduce | flops 384 | bytes 3072 | tf_op jit(solution)/shard_map/psum | solution.py:143
  337.3 2.3 constant_dynamic-slice_fusion.1
  340.2 298.8 %all-reduce.23.cloned.1.call-done = (f32[1,2,96,96]{3,2,0,1:T(8,128)}, f32[1,2,96,96]{3,2,0,1:T(8,128)}) async-done(((f32[1,2,96,96]{3,2,0,1:T(8,128)}, f32[1,2,96,96]{3,2,0,1:T(8,128)}), (f32[1,2,96,96]{3,2,0,1:T(8,128)}, f32[1,2,96,96]{3,2,0,1:T(8,128)})) %all-reduce.23.cloned.1.call-update) | async-done | bytes 147472 | tf_op jit(solution)/shard_map/psum | solution.py:143
  639.0 1.5 multiply_bitcast_fusion.1
  640.5 1.5 multiply_bitcast_fusion
  642.1 2.1 copy.128
  645.7 1.8 fusion.84
  647.6 3.3 fusion.20
  (114 shorter events, 29.1 us)
Async XLA Ops:
  7.2 1.2 copy-start
  8.4 0.7 copy-start.26
  12.4 7.7 %copy-start.8 = (bf16[1,6,100,768]{3,2,1,0:T(8,128)(2,1)S(1)}, bf16[1,6,100,768]{3,2,1,0:T(8,128)(2,1)}, u32[]{:S(2)}) copy-start(bf16[1,6,100,768]{3,2,1,0:T(8,128)(2,1)} %param.10) | copy-start | bytes 2764804
  12.4 52.4 %all-to-all-start.2 = ((f32[6,2,48,768]{3,1,0,2:T(2,128)}), f32[6,2,48,768]{3,1,0,2:T(2,128)S(1)}, u32[]{:S(2)}, u32[]{:S(2)}) async-start(f32[6,2,48,768]{3,1,0,2:T(2,128)} %copy.131), calls=%async_computation.2 | async-start | bytes 3538944 | tf_op jit(solution)/shard_map/all_to_all | solution.py:121
  20.1 0.7 copy-start.32
  27.0 42.3 %copy-start.24 = (f32[8,2,96]{2,1,0:T(2,128)S(1)}, f32[8,2,96]{2,1,0:T(2,128)}, u32[]{:S(2)}) copy-start(f32[8,2,96]{2,1,0:T(2,128)} %param.16) | copy-start | bytes 18436
  27.0 42.9 %copy-start.25 = (f32[8,2,96]{2,1,0:T(2,128)S(1)}, f32[8,2,96]{2,1,0:T(2,128)}, u32[]{:S(2)}) copy-start(f32[8,2,96]{2,1,0:T(2,128)} %param.14) | copy-start | bytes 18436
  64.8 49.1 %all-to-all-start = ((f32[6,2,48,768]{3,1,0,2:T(2,128)}), f32[6,2,48,768]{3,1,0,2:T(2,128)}, u32[]{:S(2)}, u32[]{:S(2)}) async-start(f32[6,2,48,768]{3,1,0,2:T(2,128)} %copy.108), calls=%async_computation | async-start | bytes 3538944 | tf_op jit(solution)/shard_map/all_to_all | solution.py:120
  128.8 3.4 copy-start.15
  132.2 2.3 copy-start.13
  136.4 2.8 copy-start.12
  139.2 2.6 copy-start.10
  141.8 9.3 %copy-start.2 = (f32[8,48,6,96]{3,1,2,0:T(8,128)}, f32[8,48,6,96]{3,1,2,0:T(8,128)S(1)}, u32[]{:S(2)}) copy-start(f32[8,48,6,96]{3,1,2,0:T(8,128)S(1)} %get-tuple-element.64) | copy-start | bytes 2654212
  141.8 1.7 copy-start.11
  141.8 1.9 copy-start.16
  145.2 27.8 %copy-start.4 = (f32[8,48,6,96]{3,1,2,0:T(8,128)}, f32[8,48,6,96]{3,1,2,0:T(8,128)S(1)}, u32[]{:S(2)}) copy-start(f32[8,48,6,96]{3,1,2,0:T(8,128)S(1)} %get-tuple-element.62) | copy-start | bytes 2654212
  145.2 1.7 copy-start.22
  145.2 1.7 copy-start.31
  149.9 13.4 %copy-start.6 = (f32[48,6,8,96]{3,0,1,2:T(8,128)}, f32[48,6,8,96]{3,0,1,2:T(8,128)S(1)}, u32[]{:S(2)}) copy-start(f32[48,6,8,96]{3,0,1,2:T(8,128)S(1)} %get-tuple-element.46) | copy-start | bytes 2654212
  149.9 1.7 copy-start.23
  149.9 1.7 copy-start.30
  177.3 1.9 copy-start.21
  182.6 1.3 copy-start.14
  188.6 4.5 copy-start.17
  188.6 4.5 copy-start.18
  188.6 4.5 copy-start.20
  188.6 453.4 %all-to-all-start.1 = ((f32[48,2,6,768]{3,1,2,0:T(2,128)}), f32[48,2,6,768]{3,1,2,0:T(2,128)}, u32[]{:S(2)}, u32[]{:S(2)}) async-start(f32[48,2,6,768]{3,1,2,0:T(2,128)} %copy.127), calls=%async_computation.1 | async-start | bytes 3538944 | tf_op jit(solution)/shard_map/all_to_all | solution.py:130
  193.1 2.1 copy-start.3
  193.1 144.2 %all-reduce.25.cloned.1.call-start = ((), (), s32[]{:S(2)}) async-start(), calls=%async_computation.4 | async-start | bytes 3145728
  195.2 2.5 copy-start.7
  197.7 2.5 copy-start.5
  200.2 2.5 copy-start.19
  203.7 0.7 copy-start.34
  203.7 1.3 copy-start.28
  203.7 1.3 copy-start.29
  203.7 435.3 %all-reduce.23.cloned.1.call-start = ((), (), s32[]{:S(2)}) async-start(), calls=%async_computation.3 | async-start | bytes 393216 | tf_op jit(solution)/shard_map/psum | solution.py:143
  644.2 1.5 copy-start.27
  645.7 1.8 copy-start.9
  645.7 1.8 copy-start.33
  647.6 3.3 copy-start.1
Sparse Core Ops, SparseCore 0:
  203.8 94.8 all-reduce.24
  339.8 299.1 all-reduce.22
where the time goes:
time: 668 us; the launch traced here: 658 us
  waiting for transfers between devices  371 us (56%)
  blocking collectives  131 us (20%)
  matrix products  77.9 us (12%)
  local copies, waits for them, and re-layouts  37.6 us (6%)
  starting transfers between devices  16.7 us (2%)
  between operations  15.1 us (2%)
  other arithmetic  8.74 us (1%)
    psum x1, waiting for transfers between devices, shards(): summed = lax.psum((shares[0], shares[1], shares[2], shares[3]), 'dp')  299 us
    dot_general x38, matrix products, contract(): return jnp.einsum(form, left, right, precision=lax.Precision.HIGHEST)  77.9 us
    psum x1, blocking collectives, shards(): summed = lax.psum((shares[0], shares[1], shares[2], shares[3]), 'dp')  75.4 us
    unnamed x1, blocking collectives  55.7 us
    all_to_all x1, waiting for transfers between devices, shards(): lax.all_to_all(cspec, 'space', split_axis=2, concat_axis=0, tiled=True)  37.8 us
    all_to_all x1, waiting for transfers between devices, shards(): lax.all_to_all(spec, 'space', split_axis=2, concat_axis=0, tiled=True)  34.4 us
  transfers between devices with their start and end apart: 5, of which 3 were waited for; matrix products, arithmetic and copies ran while one was open for 5% of the time, Pallas kernels for 0%

commit v1 on v0

--- a/solution.py
+++ b/solution.py
@@ -103,7 +103,11 @@
     lon_cos, lon_sin = lon_tables(width, KW)
     lat_cos, lat_sin = lat_tables(lat_rows)
     factor = mode_weights(KW)[:, None]
-    params = (weight_one, bias_one, weight_two, bias_two)
+    at = lax.axis_index("space")
+    params = tuple(
+        lax.dynamic_slice_in_dim(value, at, 1, 0)
+        for value in (weight_one, bias_one, weight_two, bias_two)
+    )
     field = members[0].astype(jnp.float32)
     normed = layer_norm(field, gain)
     spec = jnp.stack(
@@ -117,8 +121,8 @@
         ],
         1,
     )
-    spec_got = lax.all_to_all(spec, "space", split_axis=2, concat_axis=0, tiled=True)
-    cspec_got = lax.all_to_all(cspec, "space", split_axis=2, concat_axis=0, tiled=True)
+    spec_got = lax.all_to_all(spec, "space", split_axis=3, concat_axis=0, tiled=True)
+    cspec_got = lax.all_to_all(cspec, "space", split_axis=3, concat_axis=0, tiled=True)
     spec_real, spec_imag = lat_forward(spec_got[:, 0], spec_got[:, 1], lat_cos, lat_sin)
 
     def apply(first_w, first_b, second_w, second_b):
@@ -127,28 +131,22 @@
     (filt_real, filt_imag), pullback = jax.vjp(apply, *params)
     back_real, back_imag = lat_inverse(filt_real, filt_imag, lat_cos, lat_sin)
     stacked = jnp.stack([back_real, back_imag], 1)
-    returned = lax.all_to_all(stacked, "space", split_axis=0, concat_axis=2, tiled=True)
+    returned = lax.all_to_all(stacked, "space", split_axis=0, concat_axis=3, tiled=True)
     spectral = contract("kw,hkc->hwc", lon_cos * factor, returned[:, 0]) + contract(
         "kw,hkc->hwc", lon_sin * factor, returned[:, 1]
     )
     outputs = [(field + normed + spectral).astype(jnp.bfloat16)]
     dspec_real, dspec_imag = lat_forward(cspec_got[:, 0], cspec_got[:, 1], lat_cos, lat_sin)
     grads = pullback((dspec_real, dspec_imag))
-    shares = (
-        lax.psum_scatter(grads[0], "space", scatter_dimension=0, tiled=True),
-        lax.psum_scatter(grads[1], "space", scatter_dimension=0, tiled=True),
-        lax.psum_scatter(grads[2], "space", scatter_dimension=0, tiled=True),
-        lax.psum_scatter(grads[3], "space", scatter_dimension=0, tiled=True),
-    )
-    summed = lax.psum((shares[0], shares[1], shares[2], shares[3]), "dp")
+    sizes = [value.size for value in grads]
+    flat = lax.psum(jnp.concatenate([value.reshape(-1) for value in grads]), "dp")
     norm = 1.0 / math.sqrt(lax.axis_size("dp") * member_count * lat_rows * KW)
-    return (
-        jnp.stack(outputs, 0),
-        summed[0] * norm,
-        summed[1] * norm,
-        summed[2] * norm,
-        summed[3] * norm,
-    )
+    summed = []
+    start = 0
+    for value, size in zip(grads, sizes):
+        summed.append((flat[start : start + size] * norm).reshape(value.shape))
+        start += size
+    return (jnp.stack(outputs, 0), *summed)
 
 
 def solution(mesh):

time: 668 us -> 554 us (0.83)
  blocking collectives: 131 us -> 0 us
  waiting for transfers between devices: 371 us -> 327 us
  local copies, waits for them, and re-layouts: 37.6 us -> 81.6 us
  matrix products: 77.9 us -> 86.5 us
  other arithmetic: 8.74 us -> 16.8 us
    psum x1 -> x0, blocking collectives: 75.4 us -> none  [shards(): summed = lax.psum((shares[0], shares[1], shares[2], shares[3]), 'dp')]
    unnamed x1 -> x0, blocking collectives: 55.7 us -> none
    all_to_all x3, waiting for transfers between devices: 72.2 us -> 35.8 us  [the longest x1 24.8 us: shards(): lax.all_to_all(cspec, 'space', split_axis=3, concat_axis=0, tiled=True)]
    unnamed x73 -> x48, local copies, waits for them, and re-layouts: 6.81 us -> 41.5 us
    all_to_all x3 -> x5, local copies, waits for them, and re-layouts: 4.78 us -> 16.8 us  [the longest x2 6.38 us: shards(): lax.all_to_all(cspec, 'space', split_axis=3, concat_axis=0, tiled=True)]
    all_to_all x0 -> x2, other arithmetic: none -> 11.2 us  [the longest x1 6.33 us: shards(): lax.all_to_all(spec, 'space', split_axis=3, concat_axis=0, tiled=True)]
    dot_general x38, matrix products: 77.9 us -> 86.5 us  [contract(): return jnp.einsum(form, left, right, precision=lax.Precision.HIGHEST)]
    reshape x6 -> x4, local copies, waits for them, and re-layouts: 11 us -> 2.58 us  [shards(): value.reshape(-1)]
  transfers between devices with their start and end apart: 5 -> 4, of which waited for: 3 -> 3; matrix products, arithmetic and copies ran while one was open for 5% -> 16% of each run, Pallas kernels for 0% -> 0%
where the time goes in v1:
time: 554 us; the launch traced here: 544 us
  waiting for transfers between devices  327 us (59%)
  matrix products  86.5 us (16%)
  local copies, waits for them, and re-layouts  81.6 us (15%)
  starting transfers between devices  16.9 us (3%)
  other arithmetic  16.8 us (3%)
  between operations  15 us (3%)
    psum x1, waiting for transfers between devices, shards(): lax.psum(jnp.concatenate([value.reshape(-1) for value in grads]), 'dp')  292 us
    dot_general x38, matrix products, contract(): return jnp.einsum(form, left, right, precision=lax.Precision.HIGHEST)  86.5 us
    unnamed x48, local copies, waits for them, and re-layouts  41.5 us
    all_to_all x1, waiting for transfers between devices, shards(): lax.all_to_all(cspec, 'space', split_axis=3, concat_axis=0, tiled=True)  24.8 us
  transfers between devices with their start and end apart: 4, of which 3 were waited for; matrix products, arithmetic and copies ran while one was open for 16% of the time, Pallas kernels for 0%

profile of v1, /device:TPU:32, one launch (start us, length us, event | category | flops | bytes accessed | tf_op | source)
XLA Modules:
  0.0 544.3 jit_solution(2398673623171352350)
XLA Ops:
  9.8 5.3 copy.148
  15.1 10.3 %reshape.317 = f32[8,1,55296]{2,1,0:T(1,128)} reshape(f32[768,6,2,48]{3,2,1,0:T(2,128)} %bitcast.412) | data formatting | bytes 3538944
  25.4 7.7 %all-to-all-start.2 = ((f32[8,1,55296]{2,1,0:T(1,128)}), f32[8,1,55296]{2,1,0:T(1,128)S(1)}, u32[]{:S(2)}, u32[]{:S(2)}) async-start(f32[8,1,55296]{2,1,0:T(1,128)} %reshape.317), calls=%async_computation.2 | async-start | bytes 3538944 | tf_op jit(solution)/shard_map/all_to_all | solution.py:125
  33.8 1.7 fusion.27
  35.6 1.7 fusion.30
  37.4 5.3 copy.129
  42.8 10.2 %reshape.315 = f32[8,1,55296]{2,1,0:T(1,128)} reshape(f32[768,6,2,48]{3,2,1,0:T(2,128)} %bitcast.413) | data formatting | bytes 3538944
  53.0 24.8 %all-to-all-done.2 = f32[8,1,55296]{2,1,0:T(1,128)S(1)} async-done(((f32[8,1,55296]{2,1,0:T(1,128)}), f32[8,1,55296]{2,1,0:T(1,128)S(1)}, u32[]{:S(2)}, u32[]{:S(2)}) %all-to-all-start.2) | async-done | bytes 1769504 | tf_op jit(solution)/shard_map/all_to_all | solution.py:125
  77.8 4.5 all-to-all-start
  85.3 4.9 reduce.5
  90.1 9.8 %reshape.318 = f32[768,6,2,48]{3,2,1,0:T(2,128)} reshape(f32[8,55296]{1,0:T(8,128)S(1)} %reduce.5) | data formatting | bytes 3538944
  99.9 5.9 %copy.174 = f32[6,2,48,8,96]{4,2,1,0,3:T(8,128)S(1)} copy(f32[6,2,48,8,96]{2,1,0,4,3:T(2,128)} %bitcast.414) | data formatting | bytes 3538944 | tf_op jit(solution)/shard_map/all_to_all | solution.py:125
  105.9 2.5 fusion.108
  108.5 2.6 fusion.109
  111.1 2.5 fusion.110
  113.6 2.6 fusion.111
  116.2 10.9 %all-to-all-done = f32[8,1,55296]{2,1,0:T(1,128)} async-done(((f32[8,1,55296]{2,1,0:T(1,128)}), f32[8,1,55296]{2,1,0:T(1,128)}, u32[]{:S(2)}, u32[]{:S(2)}) %all-to-all-start) | async-done | bytes 1769504 | tf_op jit(solution)/shard_map/all_to_all | solution.py:124
  127.1 6.3 %reduce.6 = f32[8,55296]{1,0:T(8,128)S(1)} reduce(f32[8,1,55296]{2,1,0:T(1,128)} %all-to-all-done, f32[]{:T(128)} %broadcast.224), dimensions={1}, to_apply=%all_to_all.39.reduce_sub_computation | reduce | bytes 3538948 | tf_op jit(solution)/shard_map/all_to_all | solution.py:124
  133.4 9.9 %reshape.316 = f32[768,6,2,48]{3,2,1,0:T(2,128)} reshape(f32[8,55296]{1,0:T(8,128)S(1)} %reduce.6) | data formatting | bytes 3538944
  143.4 5.4 copy.169
  155.1 2.1 fusion.122
  157.2 2.1 fusion.128
  159.3 2.1 fusion.22
  161.5 1.9 fusion.70
  163.4 2.6 fusion.21
  166.0 2.0 fusion.66
  168.0 2.0 fusion.24
  170.2 4.6 fusion.354
  174.8 2.7 fusion.80
  177.5 2.7 fusion.85
  180.2 2.8 fusion.90
  183.0 2.7 fusion.95
  185.7 2.9 fusion.51
  195.0 2.1 copy.146
  197.2 4.4 all-to-all-start.1
  206.9 1.6 reshape.291
  208.6 2.5 fusion.53
  211.1 3.5 fusion.360
  214.6 3.0 fusion.361
  217.7 3.6 fusion.100
  221.3 2.2 fusion.103
  223.5 2.2 fusion.77
  225.7 2.5 fusion.74
  229.2 291.7 %all-reduce.14.cloned.1.call-done = f32[37248]{0:T(1024)} async-done(((f32[37248]{0:T(1024)}), f32[37248]{0:T(1024)}) %all-reduce.14.cloned.1.call-update) | async-done | bytes 149008 | tf_op jit(solution)/shard_map/psum | solution.py:142
  525.4 3.0 copy.147
  528.5 2.0 all_to_all.46
  530.5 3.1 fusion.146
  533.7 3.3 fusion.20
  (88 shorter events, 30.1 us)
Async XLA Ops:
  7.2 1.2 copy-start
  25.4 7.7 %copy-start.9 = (bf16[1,6,100,768]{3,2,1,0:T(8,128)(2,1)S(1)}, bf16[1,6,100,768]{3,2,1,0:T(8,128)(2,1)}, u32[]{:S(2)}) copy-start(bf16[1,6,100,768]{3,2,1,0:T(8,128)(2,1)} %param.10) | copy-start | bytes 2764804
  25.4 52.4 %all-to-all-start.2 = ((f32[8,1,55296]{2,1,0:T(1,128)}), f32[8,1,55296]{2,1,0:T(1,128)S(1)}, u32[]{:S(2)}, u32[]{:S(2)}) async-start(f32[8,1,55296]{2,1,0:T(1,128)} %reshape.317), calls=%async_computation.2 | async-start | bytes 3538944 | tf_op jit(solution)/shard_map/all_to_all | solution.py:125
  33.1 0.7 copy-start.17
  77.8 49.3 %all-to-all-start = ((f32[8,1,55296]{2,1,0:T(1,128)}), f32[8,1,55296]{2,1,0:T(1,128)}, u32[]{:S(2)}, u32[]{:S(2)}) async-start(f32[8,1,55296]{2,1,0:T(1,128)} %reshape.315), calls=%async_computation | async-start | bytes 3538944 | tf_op jit(solution)/shard_map/all_to_all | solution.py:124
  157.2 2.1 copy-start.20
  161.5 1.9 copy-start.19
  165.9 17.1 %copy-start.2 = (f32[1,96,48,48]{1,3,2,0:T(8,128)}, f32[1,96,48,48]{1,3,2,0:T(8,128)S(1)}, u32[]{:S(2)}) copy-start(f32[1,96,48,48]{1,3,2,0:T(8,128)S(1)} %fusion.21) | copy-start | bytes 2654212
  165.9 4.2 copy-start.15
  168.0 2.1 copy-start.12
  168.0 2.1 copy-start.13
  168.0 2.1 copy-start.14
  168.0 2.1 copy-start.21
  174.8 8.2 %copy-start.5 = (f32[48,48,1,96]{3,1,0,2:T(8,128)}, f32[48,48,1,96]{3,1,0,2:T(8,128)S(1)}, u32[]{:S(2)}) copy-start(f32[48,48,1,96]{3,1,0,2:T(8,128)S(1)} %get-tuple-element.41) | copy-start | bytes 2654212
  174.8 10.9 %copy-start.4 = (f32[48,48,1,96]{3,1,0,2:T(8,128)}, f32[48,48,1,96]{3,1,0,2:T(8,128)S(1)}, u32[]{:S(2)}) copy-start(f32[48,48,1,96]{3,1,0,2:T(8,128)S(1)} %get-tuple-element.18) | copy-start | bytes 2654212
  197.2 328.3 %all-to-all-start.1 = ((f32[48,2,48,96]{3,2,1,0:T(8,128)}), f32[48,2,48,96]{3,2,1,0:T(8,128)}, u32[]{:S(2)}, u32[]{:S(2)}) async-start(f32[48,2,48,96]{3,2,1,0:T(8,128)} %copy.146), calls=%async_computation.1 | async-start | bytes 4718592 | tf_op jit(solution)/shard_map/all_to_all | solution.py:134
  201.5 319.4 %all-reduce.14.cloned.1.call-start = ((), (), s32[]{:S(2)}) async-start(), calls=%async_computation.3 | async-start | bytes 303104 | tf_op jit(solution)/shard_map/psum | solution.py:142
  208.6 2.5 copy-start.3
  208.6 2.5 copy-start.6
  217.7 3.6 copy-start.8
  221.3 2.2 copy-start.7
  225.7 2.7 copy-start.16
  530.5 3.1 copy-start.10
  530.5 3.1 copy-start.11
  530.5 3.2 copy-start.18
  533.7 3.3 copy-start.1
Sparse Core Ops, SparseCore 0:
  229.3 291.5 all-reduce.13

commit v2 on v1

v2 whole, which is shorter than its diff:
```python
import functools
import math

import jax
import jax.numpy as jnp
import ml_dtypes
import numpy as np
from jax import lax
from jax.experimental import pallas as pl
from jax.experimental.pallas import tpu as pltpu
from jax.sharding import PartitionSpec as P

KW = 48
BS = 96
LANES = 128
TILE = 8
SHRINK = 0.01
MESH = pl.DeviceIdType.MESH
F32 = jnp.float32
BF16 = jnp.bfloat16


def halves(table):
    table = table.astype(np.float32)
    head = table.astype(ml_dtypes.bfloat16)
    tail = (table - head.astype(np.float32)).astype(ml_dtypes.bfloat16)
    return np.concatenate([head, tail], 0)


def tables(width, rows, groups):
    wavenums = np.arange(KW)
    phase = 2.0 * np.pi * (np.outer(wavenums, np.arange(width)) % width) / width
    lon = np.concatenate([np.cos(phase), -np.sin(phase)], 0) / math.sqrt(width)
    twice = np.where(wavenums == 0, 1.0, 2.0)
    twice = np.concatenate([twice, twice])[:, None]
    lats = np.arange(rows)
    phase = 2.0 * np.pi * (np.outer(lats, lats) % rows) / rows
    cos, sin = np.cos(phase) / math.sqrt(rows), -np.sin(phase) / math.sqrt(rows)
    lat = np.block([[cos, -sin], [sin, cos]])
    local = rows // groups
    order = [
        part * rows + at * local + 2 * pair + second
        for pair in range(local // 2)
        for part in range(2)
        for second in range(2)
        for at in range(groups)
    ]
    lat = lat[:, order]
    return (
        halves(lon),
        halves(lon * twice),
        halves(lat),
        np.ascontiguousarray(lat.T).astype(ml_dtypes.bfloat16),
        np.ascontiguousarray((lon * twice).T).astype(ml_dtypes.bfloat16),
    )


def split(value):
    head = value.astype(BF16)
    return head, (value - head.astype(F32)).astype(BF16)


def dot(left, right, dims=((1,), (0,))):
    return lax.dot_general(left, right, (dims, ((), ())), preferred_element_type=F32)


def dot3(left, right, dims=((1,), (0,))):
    return dot(left[0], right[0], dims) + (
        dot(left[0], right[1], dims) + dot(left[1], right[0], dims)
    )


def unpack(lane, three):
    first, second, third = three
    return (
        first,
        pltpu.roll(jnp.where(lane >= 96, first, second), 32, 1),
        pltpu.roll(jnp.where(lane >= 64, second, third), 64, 1),
        pltpu.roll(third, 96, 1),
    )


def pack(lane, four):
    first = four[0]
    second, third, fourth = (pltpu.roll(four[i], 128 - 32 * i, 1) for i in (1, 2, 3))
    return (
        jnp.where(lane < 96, first, second),
        jnp.where(lane < 64, second, third),
        jnp.where(lane < 32, third, fourth),
    )


def exchange(lane, rows):
    pieces = [unpack(lane, row) for row in rows]
    return [pack(lane, [piece[place] for piece in pieces]) for place in range(4)]


def kernel(
    groups, team, norm,
    mem, cot, gain, w1, b1, w2, b2, lonf, lonc, latf, lati, loni,
    mixed, gw1, gb1, gw2, gb2,
    vmem, vcot, base, lon, wraw, wa, wb, spec, first, mask, sums, biases,
    sa, ra, sb, rb, sc, rc, part, parts, total, done,
    insem, outsem, locsem, sas, ras, sbs, rbs, scs, rcs, ps, pr, ts, tr,
):
    me = lax.axis_index("space")
    member = lax.axis_index("dp")
    pairs = 3
    width = vmem.shape[1]
    lane = lax.broadcasted_iota(jnp.int32, (8, LANES), 1)

    loads = [
        pltpu.make_async_copy(mem.at[0], vmem, insem.at[0]),
        pltpu.make_async_copy(cot.at[0], vcot, insem.at[1]),
        pltpu.make_async_copy(w1.at[me], wraw.at[0], insem.at[2]),
        pltpu.make_async_copy(w2.at[me], wraw.at[1], insem.at[3]),
    ]
    for load in loads:
        load.start()

    barrier = pltpu.get_barrier_semaphore()

    def greet(axis, size, at):
        def one(i, carry):
            pl.semaphore_signal(
                barrier, inc=1, device_id={axis: lax.rem(at + i, size)}, device_id_type=MESH
            )
            return carry

        lax.fori_loop(1, size, one, 0)

    greet("space", groups, me)
    greet("dp", team, member)

    def block(chunk, at):
        return pl.ds(pl.multiple_of((chunk * groups + at) * 144, 144), 144)

    def remote(src, dst, send, recv, chunk, i):
        to = lax.rem(me + i, groups)
        return pltpu.make_async_remote_copy(
            src_ref=src.at[block(chunk, to)],
            dst_ref=dst.at[block(chunk, me)],
            send_sem=send.at[chunk, i],
            recv_sem=recv.at[chunk, i],
            device_id={"space": to},
            device_id_type=MESH,
        )

    def own(src, dst, which, chunk):
        return pltpu.make_async_copy(
            src.at[block(chunk, me)], dst.at[block(chunk, me)], locsem.at[which, chunk]
        )

    def send(src, dst, sends, recvs, which, chunk):
        def one(i, carry):
            remote(src, dst, sends, recvs, chunk, i).start()
            return carry

        lax.fori_loop(1, groups, one, 0)
        own(src, dst, which, chunk).start()

    def sent(src, dst, sends, recvs, chunk):
        def one(i, carry):
            remote(src, dst, sends, recvs, chunk, i).wait_send()
            return carry

        lax.fori_loop(1, groups, one, 0)

    def received(src, dst, sends, recvs, which, chunk):
        def one(i, carry):
            remote(src, dst, sends, recvs, chunk, i).wait_recv()
            return carry

        lax.fori_loop(1, groups, one, 0)
        own(src, dst, which, chunk).wait()

    a_way = (sa, ra, sas, ras)
    b_way = (sb, rb, sbs, rbs)
    c_way = (sc, rc, scs, rcs)

    loads[0].wait()

    def out_rows(pair, place):
        def one(step, carry):
            low = pl.ds(pl.multiple_of(step * 8, 8), 8)
            high = pl.ds(pl.multiple_of(48 + step * 8, 8), 8)
            for group in range(2):
                cols = [pl.ds(group * 384 + 128 * v, 128) for v in range(3)]
                rows = [
                    [lon[second, ks, col] for col in cols]
                    for ks in (low, high)
                    for second in range(2)
                ]
                for b, three in enumerate(exchange(lane, rows)):
                    for v in range(3):
                        place(step, 4 * group + b, v, three[v])
            return carry

        lax.fori_loop(0, 6, one, 0)

    def forward_pair(pair, carry):
        for second in range(2):
            row = 2 * pair + second
            field = vmem[row].astype(F32)
            center = field - jnp.mean(field, axis=-1, keepdims=True)
            spread = jnp.mean(center * center, axis=-1, keepdims=True) + 1e-05
            inverse = lax.rsqrt(spread)
            inverse = inverse * (1.5 - 0.5 * spread * inverse * inverse)
            normed = center * inverse * gain[...]
            base[row] = field + normed
            head, tail = split(normed)
            both = dot(lonf[...], head)
            lon[second] = both[:96] + (both[96:] + dot(lonf[:96], tail))

        def place(step, to, v, value):
            at = ((pair * groups + to) * 3 + v) * 48 + step * 8
            sa[pl.ds(pl.multiple_of(at, 8), 8), :] = value

        out_rows(pair, place)

        @pl.when(pair == 0)
        def _():
            pl.semaphore_wait(barrier, groups - 1 + team - 1)

        send(*a_way, 0, pair)
        return carry

    lax.fori_loop(0, pairs, forward_pair, 0)

    loads[1].wait()

    def cot_pair(pair, carry):
        for second in range(2):
            both = dot(lonc[...], vcot[2 * pair + second])
            lon[second] = both[:96] + both[96:]

        def place(step, to, v, value):
            at = ((step // 2 * groups + to) * 9 + pair * 3 + v) * 16 + lax.rem(step, 2) * 8
            sb[pl.ds(pl.multiple_of(at, 8), 8), :] = value

        out_rows(pair, place)
        return carry

    lax.fori_loop(0, pairs, cot_pair, 0)

    loads[2].wait()
    loads[3].wait()
    for which, held in ((0, wa), (1, wb)):
        held[...] = jnp.zeros_like(held)
        real, imag = split(wraw[which, 0]), split(wraw[which, 1])
        for i in range(2):
            held[i, 0:BS, 0:BS] = real[i]
            held[i, 0:BS, 128 : 128 + BS] = imag[i]
            held[i, 128 : 128 + BS, 0:BS] = -imag[i]
            held[i, 128 : 128 + BS, 128 : 128 + BS] = real[i]
    biases[...] = jnp.zeros_like(biases)
    for which, ref in ((0, b1), (1, b2)):
        value = ref[me]
        biases[which : which + 1, 0:BS] = value[0:1]
        biases[which : which + 1, 128 : 128 + BS] = value[1:2]
    sums[...] = jnp.zeros_like(sums)
    part[...] = jnp.zeros_like(part)

    for chunk in range(3):
        sent(*a_way, chunk)
        send(*b_way, 1, chunk)
    for chunk in range(3):
        received(*a_way, 0, chunk)

    def columns(ref, start):
        pieces = []
        for pair in range(pairs):
            three = [ref[pl.ds(start(pair, v), groups, stride=144), :] for v in range(3)]
            pieces += unpack(lane, three)
        return jnp.concatenate(pieces, 0)

    def latitude(ref, start, k):
        held = jnp.concatenate(
            [columns(ref, lambda p, v, k=k + i: start(p, v, k)) for i in range(2)], 1
        )
        head, tail = split(held)
        both = dot(latf[...], head)
        out = both[:96] + (both[96:] + dot(latf[:96], tail))
        return [
            jnp.concatenate([out[:48, at : at + 128], out[48:, at : at + 128]], 1)
            for at in (0, 128)
        ]

    def modes(ref, start, k):
        found = []
        for i in range(0, TILE, 2):
            found += latitude(ref, start, k + i)
        return jnp.concatenate(found, 0)

    def filter_tile(tile, carry):
        k = tile * TILE
        here = pl.ds(pl.multiple_of(k * 48, 48 * TILE), 48 * TILE)
        value = modes(ra, lambda p, v, k: (p * groups * 3 + v) * 48 + k, k)
        head, tail = split(value)
        spec[0, here, :] = head
        spec[1, here, :] = tail
        one = jnp.maximum(dot3((head, tail), (wa[0], wa[1])) + biases[0:1, :], 0.0)
        head, tail = split(one)
        first[0, here, :] = head
        first[1, here, :] = tail
        two = dot3((head, tail), (wb[0], wb[1])) + biases[1:2, :]
        size = jnp.abs(two)
        mask[here, :] = jnp.where(
            size > SHRINK, 1.0, jnp.where(size == SHRINK, 0.5, 0.0)
        ).astype(BF16)
        kept = (two - jnp.clip(two, -SHRINK, SHRINK)).astype(BF16)
        for i in range(0, TILE, 2):
            held = jnp.concatenate(
                [
                    jnp.concatenate([kept[at : at + 48, :128], kept[at : at + 48, 128:]], 0)
                    for at in (48 * i, 48 * i + 48)
                ],
                1,
            )
            back = dot(lati[...], held)
            for second in range(2):
                for pair in range(pairs):
                    four = [
                        back[
                            pair * 32 + 8 * a : pair * 32 + 8 * a + 8,
                            128 * second : 128 * second + 128,
                        ]
                        for a in range(4)
                    ]
                    for v, value in enumerate(pack(lane, four)):
                        at = (pair * groups * 3 + v) * 48 + k + i + second
                        sc[pl.ds(at, groups, stride=144), :] = value
        return carry

    lax.fori_loop(0, KW // TILE, filter_tile, 0)

    def grad_tile(tile, carry):
        k = tile * TILE
        here = pl.ds(pl.multiple_of(k * 48, 48 * TILE), 48 * TILE)

        def start(p, v, k):
            third = k // 16
            return (third * groups * 9 + p * 3 + v) * 16 + (k - third * 16)

        two = modes(rb, start, k) * mask[here, :].astype(F32)
        sums[2, 0:1, :] += jnp.sum(two, axis=0, keepdims=True)
        two = split(two)
        held = (first[0, here, :], first[1, here, :])
        sums[1] += dot3(held, two, ((0,), (0,)))
        one = dot3(two, (wb[0], wb[1]), ((1,), (1,)))
        one = jnp.where(held[0] > 0, one, 0.0)
        sums[2, 8:9, :] += jnp.sum(one, axis=0, keepdims=True)
        sums[0] += dot3((spec[0, here, :], spec[1, here, :]), split(one), ((0,), (0,)))
        return carry

    per = KW // TILE // 3
    for chunk in range(3):
        received(*b_way, 1, chunk)
        if chunk == 2:
            for third in range(3):
                sent(*b_way, third)
            for pair in range(pairs):
                send(*c_way, 2, pair)
        lax.fori_loop(chunk * per, chunk * per + per, grad_tile, 0)

    for which in range(2):
        held = sums.at[which]
        part[192 * which : 192 * which + 96, :] = held[0:96, 0:128] + held[128:224, 128:256]
        part[192 * which + 96 : 192 * which + 192, :] = (
            held[0:96, 128:256] - held[128:224, 0:128]
        )
    for i, row in enumerate((8, 0)):
        part[384 + 2 * i : 385 + 2 * i, :] = sums[2, row : row + 1, 0:128]
        part[385 + 2 * i : 386 + 2 * i, :] = sums[2, row : row + 1, 128:256]

    share = part.shape[0] // team

    def rows_of(at):
        return pl.ds(pl.multiple_of(at * share, share), share)

    def scatter(i):
        to = lax.rem(member + i, team)
        return pltpu.make_async_remote_copy(
            src_ref=part.at[rows_of(to)],
            dst_ref=parts.at[rows_of(i)],
            send_sem=ps.at[i],
            recv_sem=pr.at[i],
            device_id={"dp": to},
            device_id_type=MESH,
        )

    def gather(i):
        to = lax.rem(member + i, team)
        return pltpu.make_async_remote_copy(
            src_ref=total,
            dst_ref=done.at[rows_of(member)],
            send_sem=ts.at[i],
            recv_sem=tr.at[i],
            device_id={"dp": to},
            device_id_type=MESH,
        )

    def each(function):
        def one(i, carry):
            function(i)
            return carry

        lax.fori_loop(1, team, one, 0)

    each(lambda i: scatter(i).start())

    def add(i, value):
        scatter(i).wait_recv()
        return value + parts[rows_of(i), :]

    total[...] = lax.fori_loop(1, team, add, part[rows_of(member), :]) * norm
    each(lambda i: gather(i).start())
    done[rows_of(member), :] = total[...]
    each(lambda i: gather(i).wait_recv())
    for which, held in ((0, gw1), (1, gw2)):
        held[0, 0] = done[192 * which : 192 * which + 96, 0:BS]
        held[0, 1] = done[192 * which + 96 : 192 * which + 192, 0:BS]
    gb1[0] = done[384:386, 0:BS]
    gb2[0] = done[386:388, 0:BS]

    def stored(pair):
        return pltpu.make_async_copy(
            vmem.at[pl.ds(2 * pair, 2)], mixed.at[0, pl.ds(2 * pair, 2)], outsem.at[pair]
        )

    for pair in range(pairs):
        received(*c_way, 2, pair)

        def one(step, carry, pair=pair):
            for group in range(2):
                rows = [
                    [
                        rc[
                            pl.ds(
                                pl.multiple_of(
                                    ((pair * groups + 4 * group + b) * 3 + v) * 48 + step * 8, 8
                                ),
                                8,
                            ),
                            :,
                        ]
                        for v in range(3)
                    ]
                    for b in range(4)
                ]
                for a, three in enumerate(exchange(lane, rows)):
                    ks = pl.ds(pl.multiple_of((a // 2) * 48 + step * 8, 8), 8)
                    for v in range(3):
                        lon[a % 2, ks, group * 384 + 128 * v : group * 384 + 128 * v + 128] = (
                            three[v]
                        )
            return carry

        lax.fori_loop(0, 6, one, 0)
        for second in range(2):
            row = 2 * pair + second
            spectral = dot(loni[...], lon[second].astype(BF16))
            vmem[row] = (base[row] + spectral).astype(BF16)
        stored(pair).start()

    for pair in range(pairs):
        sent(*c_way, pair)
        stored(pair).wait()
    each(lambda i: scatter(i).wait_send())
    each(lambda i: gather(i).wait_send())


def solution(mesh):
    groups, team = mesh.shape["space"], mesh.shape["dp"]

    def shards(members, cotangent, gain, weight_one, bias_one, weight_two, bias_two):
        _, rows, width, channels = members.shape
        norm = 1.0 / math.sqrt(team * members.shape[0] * rows * groups * KW)
        made = tables(width, rows * groups, groups)
        moved = pltpu.VMEM((3 * groups * 144, LANES), F32)
        share = -(-400 // (team * 8)) * 8
        sems = pltpu.SemaphoreType.DMA((3, groups))
        team_sems = pltpu.SemaphoreType.DMA((team,))
        modes = KW * rows * groups
        whole = pl.BlockSpec(memory_space=pltpu.VMEM)
        away = pl.BlockSpec(memory_space=pl.ANY)
        return pl.pallas_call(
            functools.partial(kernel, groups, team, norm),
            out_shape=(
                jax.ShapeDtypeStruct(members.shape, BF16),
                jax.ShapeDtypeStruct((1,) + weight_one.shape[1:], F32),
                jax.ShapeDtypeStruct((1,) + bias_one.shape[1:], F32),
                jax.ShapeDtypeStruct((1,) + weight_two.shape[1:], F32),
                jax.ShapeDtypeStruct((1,) + bias_two.shape[1:], F32),
            ),
            in_specs=[away, away, whole, away, whole, away, whole] + [whole] * 5,
            out_specs=(away, whole, whole, whole, whole),
            scratch_shapes=[
                pltpu.VMEM((rows, width, channels), BF16),
                pltpu.VMEM((rows, width, channels), BF16),
                pltpu.VMEM((rows, width, channels), F32),
                pltpu.VMEM((2, 2 * KW, channels), F32),
                pltpu.VMEM((2, 2, BS, BS), F32),
                pltpu.VMEM((2, 256, 256), BF16),
                pltpu.VMEM((2, 256, 256), BF16),
                pltpu.VMEM((2, modes, 256), BF16),
                pltpu.VMEM((2, modes, 256), BF16),
                pltpu.VMEM((modes, 256), BF16),
                pltpu.VMEM((3, 256, 256), F32),
                pltpu.VMEM((8, 256), F32),
                moved, moved, moved, moved, moved, moved,
                pltpu.VMEM((share * team, LANES), F32),
                pltpu.VMEM((share * team, LANES), F32),
                pltpu.VMEM((share, LANES), F32),
                pltpu.VMEM((share * team, LANES), F32),
                pltpu.SemaphoreType.DMA((4,)),
                pltpu.SemaphoreType.DMA((3,)),
                pltpu.SemaphoreType.DMA((3, 3)),
                sems, sems, sems, sems, sems, sems,
                team_sems, team_sems, team_sems, team_sems,
            ],
            compiler_params=pltpu.CompilerParams(
                collective_id=0, has_side_effects=True, vmem_limit_bytes=56 << 20
            ),
            name="afno_block",
        )(
            members, cotangent, gain.reshape(1, -1), weight_one, bias_one, weight_two, bias_two,
            *made,
        )

    in_specs = (P("dp", "space", None, None), P("dp", "space", None, None), P(), P(), P(), P(), P())
    out_specs = (
        P("dp", "space", None, None),
        P("space", None, None, None),
        P("space", None, None),
        P("space", None, None, None),
        P("space", None, None),
    )
    return jax.shard_map(shards, mesh=mesh, in_specs=in_specs, out_specs=out_specs, check_vma=False)
```

time: 554 us -> 155 us (0.28); the launches traced: 544 us -> 154 us
  waiting for transfers between devices: 327 us -> 0 us
  Pallas kernels: 0 us -> 147 us
  matrix products: 86.5 us -> 0 us
  local copies, waits for them, and re-layouts: 81.6 us -> 5.98 us
  starting transfers between devices: 16.9 us -> 0 us
  other arithmetic: 16.8 us -> 0 us
  between operations: 15 us -> 0.65 us
    psum x1 -> x0, waiting for transfers between devices: 292 us -> none  [shards(): lax.psum(jnp.concatenate([value.reshape(-1) for value in grads]), 'dp')]
    pallas_call x0 -> x1, Pallas kernels: none -> 147 us  [shards(): pl.pallas_call(functools.partial(kernel, groups, team, norm), out_shape=(...]
    dot_general x38 -> x0, matrix products: 86.5 us -> none  [contract(): return jnp.einsum(form, left, right, precision=lax.Precision.HIGHEST)]
    unnamed x48 -> x13, local copies, waits for them, and re-layouts: 41.5 us -> 4.71 us
    all_to_all x3 -> x0, waiting for transfers between devices: 35.8 us -> none  [the longest x1 24.8 us: shards(): lax.all_to_all(cspec, 'space', split_axis=3, concat_axis=0, tiled=True)]
    all_to_all x5 -> x0, local copies, waits for them, and re-layouts: 16.8 us -> none  [the longest x2 6.38 us: shards(): lax.all_to_all(cspec, 'space', split_axis=3, concat_axis=0, tiled=True)]
    all_to_all x3 -> x0, starting transfers between devices: 16.6 us -> none  [the longest x1 7.7 us: shards(): lax.all_to_all(cspec, 'space', split_axis=3, concat_axis=0, tiled=True)]
    another operation x3 -> x0, local copies, waits for them, and re-layouts: 12.8 us -> none  [the longest x1 5.35 us: shards(): jnp.stack([contract('kw,hwc->hkc', lon_cos * factor, cot), contract('kw,h...]
  transfers between devices with their start and end apart: 4 -> 0, of which waited for: 3 -> 0; matrix products, arithmetic and copies ran while one was open for 16% -> 0% of each run, Pallas kernels for 0% -> 0%
where the time goes in v2:
time: 155 us; the launch traced here: 154 us
  Pallas kernels  147 us (95%)
  local copies, waits for them, and re-layouts  5.98 us (4%)
    pallas_call x1, Pallas kernels, shards(): pl.pallas_call(functools.partial(kernel, groups, team, norm), out_shape=(...  147 us
    unnamed x13, local copies, waits for them, and re-layouts  4.71 us

profile of v2, /device:TPU:32, one launch (start us, length us, event | category | flops | bytes accessed | tf_op | source)
XLA Modules:
  0.0 153.6 jit_solution(10240539255059523898)
XLA Ops:
  0.6 1.3 reshape.13.gain
  1.9 147.0 %afno_block.1 = (bf16[1,6,100,768]{3,2,1,0:T(8,128)(2,1)}, f32[1,2,96,96]{3,2,1,0:T(8,128)}, f32[1,2,96]{2,1,0:T(2,128)}, f32[1,2,96,96]{3,2,1,0:T(8,128)}, f32[1,2,96]{2,1,0:T(2,128)}) custom-call(bf16[1,6,100,768]{3,2,1,0:T(8,128)(2,1)} %mem.1, bf16[1,6,100,768]{3,2,1,0:T(8,128)(2,1)} %cot.1, f32[1,768]{1,0:T(1,128)} %reshape.13.gain, ...), custom_call_target="tpu_custom_call" | custom-call | tf_op jit(solution)/shard_map/afno_block/pallas_call | solution.py:487
  148.9 0.0 copy-start.1
  148.9 2.2 %copy.22 = bf16[1,6,100,768]{3,2,1,0:T(8,128)(2,1)} copy(bf16[1,6,100,768]{3,2,1,0:T(8,128)(2,1)} %get-tuple-element.10) | data formatting | bytes 1843200
  151.1 0.0 copy-done.1
  151.1 0.0 copy-start.3
  151.1 0.0 copy-start
  151.1 0.6 copy.23
  151.8 0.0 copy-done.3
  151.8 0.6 copy.24
  152.4 0.0 copy-done
  152.4 0.0 copy-start.2
  152.4 0.6 copy.25
  153.0 0.0 copy-done.2
  153.0 0.6 copy.26
Async XLA Ops:
  148.9 2.2 %copy-start.1 = (f32[1,2,96,96]{3,2,1,0:T(8,128)S(1)}, f32[1,2,96,96]{3,2,1,0:T(8,128)}, u32[]{:S(2)}) copy-start(f32[1,2,96,96]{3,2,1,0:T(8,128)} %get-tuple-element.11) | copy-start | bytes 221188
  151.1 0.7 copy-start.3
  151.1 1.2 copy-start
  152.4 0.7 copy-start.2

commit v3 on v2

--- a/solution.py
+++ b/solution.py
@@ -98,10 +98,10 @@
 def kernel(
     groups, team, norm,
     mem, cot, gain, w1, b1, w2, b2, lonf, lonc, latf, lati, loni,
-    mixed, gw1, gb1, gw2, gb2,
+    mixed, grads,
     vmem, vcot, base, lon, wraw, wa, wb, spec, first, mask, sums, biases,
     sa, ra, sb, rb, sc, rc, part, parts, total, done,
-    insem, outsem, locsem, sas, ras, sbs, rbs, scs, rcs, ps, pr, ts, tr,
+    insem, outsem, donesem, locsem, sas, ras, sbs, rbs, scs, rcs, ps, pr, ts, tr,
 ):
     me = lax.axis_index("space")
     member = lax.axis_index("dp")
@@ -206,7 +206,7 @@
             spread = jnp.mean(center * center, axis=-1, keepdims=True) + 1e-05
             inverse = lax.rsqrt(spread)
             inverse = inverse * (1.5 - 0.5 * spread * inverse * inverse)
-            normed = center * inverse * gain[...]
+            normed = center * inverse * gain[...].reshape(1, -1)
             base[row] = field + normed
             head, tail = split(normed)
             both = dot(lonf[...], head)
@@ -359,8 +359,7 @@
         if chunk == 2:
             for third in range(3):
                 sent(*b_way, third)
-            for pair in range(pairs):
-                send(*c_way, 2, pair)
+            send(*c_way, 2, 0)
         lax.fori_loop(chunk * per, chunk * per + per, grad_tile, 0)
 
     for which in range(2):
@@ -408,6 +407,7 @@
         lax.fori_loop(1, team, one, 0)
 
     each(lambda i: scatter(i).start())
+    send(*c_way, 2, 1)
 
     def add(i, value):
         scatter(i).wait_recv()
@@ -415,18 +415,15 @@
 
     total[...] = lax.fori_loop(1, team, add, part[rows_of(member), :]) * norm
     each(lambda i: gather(i).start())
+    send(*c_way, 2, 2)
     done[rows_of(member), :] = total[...]
-    each(lambda i: gather(i).wait_recv())
-    for which, held in ((0, gw1), (1, gw2)):
-        held[0, 0] = done[192 * which : 192 * which + 96, 0:BS]
-        held[0, 1] = done[192 * which + 96 : 192 * which + 192, 0:BS]
-    gb1[0] = done[384:386, 0:BS]
-    gb2[0] = done[386:388, 0:BS]
 
     def stored(pair):
         return pltpu.make_async_copy(
             vmem.at[pl.ds(2 * pair, 2)], mixed.at[0, pl.ds(2 * pair, 2)], outsem.at[pair]
         )
+
+    summed = pltpu.make_async_copy(done, grads, donesem)
 
     for pair in range(pairs):
         received(*c_way, 2, pair)
@@ -462,12 +459,34 @@
             spectral = dot(loni[...], lon[second].astype(BF16))
             vmem[row] = (base[row] + spectral).astype(BF16)
         stored(pair).start()
+        if pair == 1:
+            each(lambda i: gather(i).wait_recv())
+            summed.start()
 
     for pair in range(pairs):
         sent(*c_way, pair)
         stored(pair).wait()
     each(lambda i: scatter(i).wait_send())
     each(lambda i: gather(i).wait_send())
+    summed.wait()
+
+
+def handover(mixed, grads, out, gw1, gb1, gw2, gb2, held, insem, outsem):
+    rows = held.shape[0]
+    loads = [pltpu.make_async_copy(mixed.at[0, i], held.at[i], insem.at[i]) for i in range(rows)]
+    stores = [pltpu.make_async_copy(held.at[i], out.at[0, i], outsem.at[i]) for i in range(rows)]
+    for load in loads:
+        load.start()
+    for which, ref in ((0, gw1), (1, gw2)):
+        ref[0, 0] = grads[192 * which : 192 * which + 96, 0:BS]
+        ref[0, 1] = grads[192 * which + 96 : 192 * which + 192, 0:BS]
+    gb1[0] = grads[384:386, 0:BS]
+    gb2[0] = grads[386:388, 0:BS]
+    for load, store in zip(loads, stores):
+        load.wait()
+        store.start()
+    for store in stores:
+        store.wait()
 
 
 def solution(mesh):
@@ -484,17 +503,14 @@
         modes = KW * rows * groups
         whole = pl.BlockSpec(memory_space=pltpu.VMEM)
         away = pl.BlockSpec(memory_space=pl.ANY)
-        return pl.pallas_call(
+        mixed, grads = pl.pallas_call(
             functools.partial(kernel, groups, team, norm),
             out_shape=(
                 jax.ShapeDtypeStruct(members.shape, BF16),
-                jax.ShapeDtypeStruct((1,) + weight_one.shape[1:], F32),
-                jax.ShapeDtypeStruct((1,) + bias_one.shape[1:], F32),
-                jax.ShapeDtypeStruct((1,) + weight_two.shape[1:], F32),
-                jax.ShapeDtypeStruct((1,) + bias_two.shape[1:], F32),
+                jax.ShapeDtypeStruct((share * team, LANES), F32),
             ),
             in_specs=[away, away, whole, away, whole, away, whole] + [whole] * 5,
-            out_specs=(away, whole, whole, whole, whole),
+            out_specs=(away, away),
             scratch_shapes=[
                 pltpu.VMEM((rows, width, channels), BF16),
                 pltpu.VMEM((rows, width, channels), BF16),
@@ -515,6 +531,7 @@
                 pltpu.VMEM((share * team, LANES), F32),
                 pltpu.SemaphoreType.DMA((4,)),
                 pltpu.SemaphoreType.DMA((3,)),
+                pltpu.SemaphoreType.DMA,
                 pltpu.SemaphoreType.DMA((3, 3)),
                 sems, sems, sems, sems, sems, sems,
                 team_sems, team_sems, team_sems, team_sems,
@@ -524,9 +541,27 @@
             ),
             name="afno_block",
         )(
-            members, cotangent, gain.reshape(1, -1), weight_one, bias_one, weight_two, bias_two,
+            members, cotangent, gain, weight_one, bias_one, weight_two, bias_two,
             *made,
         )
+        return pl.pallas_call(
+            handover,
+            out_shape=(
+                jax.ShapeDtypeStruct(members.shape, BF16),
+                jax.ShapeDtypeStruct((1,) + weight_one.shape[1:], F32),
+                jax.ShapeDtypeStruct((1,) + bias_one.shape[1:], F32),
+                jax.ShapeDtypeStruct((1,) + weight_two.shape[1:], F32),
+                jax.ShapeDtypeStruct((1,) + bias_two.shape[1:], F32),
+            ),
+            in_specs=[away, whole],
+            out_specs=(away, whole, whole, whole, whole),
+            scratch_shapes=[
+                pltpu.VMEM((rows, width, channels), BF16),
+                pltpu.SemaphoreType.DMA((rows,)),
+                pltpu.SemaphoreType.DMA((rows,)),
+            ],
+            name="handover",
+        )(mixed, grads)
 
     in_specs = (P("dp", "space", None, None), P("dp", "space", None, None), P(), P(), P(), P(), P())
     out_specs = (

time: 155 us -> 143 us (0.923)
  Pallas kernels: 147 us -> 140 us
  local copies, waits for them, and re-layouts: 5.98 us -> 0 us
    pallas_call x1, Pallas kernels: 147 us -> 136 us  [shards(): pl.pallas_call(functools.partial(kernel, groups, team, norm), out_shape=(...]
    unnamed x13 -> x0, local copies, waits for them, and re-layouts: 4.71 us -> none
    pallas_call x0 -> x1, Pallas kernels: none -> 3.68 us  [shards(): pl.pallas_call(handover, out_shape=(jax.ShapeDtypeStruct(members.shape, B...]
where the time goes in v3:
time: 143 us; the launch traced here: 141 us
  Pallas kernels  140 us (98%)
    pallas_call x1, Pallas kernels, shards(): pl.pallas_call(functools.partial(kernel, groups, team, norm), out_shape=(...  136 us
    pallas_call x1, Pallas kernels, shards(): pl.pallas_call(handover, out_shape=(jax.ShapeDtypeStruct(members.shape, B...  3.68 us

profile of v3, /device:TPU:32, one launch (start us, length us, event | category | flops | bytes accessed | tf_op | source)
XLA Modules:
  0.0 140.8 jit_solution(17390816114443074306)
XLA Ops:
  0.6 136.5 %afno_block.1 = (bf16[1,6,100,768]{3,2,1,0:T(8,128)(2,1)}, f32[512,128]{1,0:T(8,128)}) custom-call(bf16[1,6,100,768]{3,2,1,0:T(8,128)(2,1)} %mem.1, bf16[1,6,100,768]{3,2,1,0:T(8,128)(2,1)} %cot.1, f32[768]{0:T(1024)} %gain.1, f32[8,2,96,96]{3,2,1,0:T(8,128)} %w1.1, f32[8,2,96]{2,1,0:T(2,128)} %b1.1, f32[8,2,96,96]{3,2,1,0:T(8,128)} %w2.1, f32[8,2,96]{2,1,0:T(2,128)} %b2.1, ...), custom_call_target="tpu_custom_call" | custom-call | tf_op jit(solution)/shard_map/afno_block/pallas_call | solution.py:506
  137.1 3.7 %handover.1 = (bf16[1,6,100,768]{3,2,1,0:T(8,128)(2,1)}, f32[1,2,96,96]{3,2,1,0:T(8,128)}, f32[1,2,96]{2,1,0:T(2,128)}, f32[1,2,96,96]{3,2,1,0:T(8,128)}, f32[1,2,96]{2,1,0:T(2,128)}) custom-call(bf16[1,6,100,768]{3,2,1,0:T(8,128)(2,1)} %get-tuple-element.7.mixed, f32[512,128]{1,0:T(8,128)} %get-tuple-element.8.grads), custom_call_target="tpu_custom_call" | custom-call | tf_op jit(solution)/shard_map/handover/pallas_call | solution.py:547

commit v4 on v3

--- a/solution.py
+++ b/solution.py
@@ -101,7 +101,7 @@
     mixed, grads,
     vmem, vcot, base, lon, wraw, wa, wb, spec, first, mask, sums, biases,
     sa, ra, sb, rb, sc, rc, part, parts, total, done,
-    insem, outsem, donesem, locsem, sas, ras, sbs, rbs, scs, rcs, ps, pr, ts, tr,
+    insem, outsem, donesem, locsem, sas, ras, sbs, rbs, scs, rcs, ps, pr, zs, zr, ts, tr,
 ):
     me = lax.axis_index("space")
     member = lax.axis_index("dp")
@@ -109,28 +109,43 @@
     width = vmem.shape[1]
     lane = lax.broadcasted_iota(jnp.int32, (8, LANES), 1)
 
+    def loaded(pair):
+        two = pl.ds(2 * pair, 2)
+        return pltpu.make_async_copy(mem.at[0, two], vmem.at[two], insem.at[pair])
+
     loads = [
-        pltpu.make_async_copy(mem.at[0], vmem, insem.at[0]),
-        pltpu.make_async_copy(cot.at[0], vcot, insem.at[1]),
-        pltpu.make_async_copy(w1.at[me], wraw.at[0], insem.at[2]),
-        pltpu.make_async_copy(w2.at[me], wraw.at[1], insem.at[3]),
+        pltpu.make_async_copy(cot.at[0], vcot, insem.at[3]),
+        pltpu.make_async_copy(w1.at[me], wraw.at[0], insem.at[4]),
+        pltpu.make_async_copy(w2.at[me], wraw.at[1], insem.at[5]),
     ]
+    for pair in range(pairs):
+        loaded(pair).start()
     for load in loads:
         load.start()
 
     barrier = pltpu.get_barrier_semaphore()
 
-    def greet(axis, size, at):
+    def greet(axis, peer, size):
         def one(i, carry):
-            pl.semaphore_signal(
-                barrier, inc=1, device_id={axis: lax.rem(at + i, size)}, device_id_type=MESH
-            )
+            pl.semaphore_signal(barrier, inc=1, device_id={axis: peer(i)}, device_id_type=MESH)
             return carry
 
         lax.fori_loop(1, size, one, 0)
 
-    greet("space", groups, me)
-    greet("dp", team, member)
+    plane = team // 2
+    inner = min(4, plane)
+    side = lax.rem(lax.div(member, inner), 2)
+    flat = lax.div(member, 2 * inner) * inner + lax.rem(member, inner)
+    twin = member + inner * (1 - 2 * side)
+
+    def mate(i):
+        at = lax.rem(flat + i, plane)
+        return lax.div(at, inner) * (2 * inner) + side * inner + lax.rem(at, inner)
+
+    greet("space", lambda i: lax.rem(me + i, groups), groups)
+    greet("dp", mate, plane)
+    greet("dp", lambda i: twin, 2)
+    greeted = groups - 1 + plane - 1 + 1
 
     def block(chunk, at):
         return pl.ds(pl.multiple_of((chunk * groups + at) * 144, 144), 144)
@@ -151,13 +166,14 @@
             src.at[block(chunk, me)], dst.at[block(chunk, me)], locsem.at[which, chunk]
         )
 
-    def send(src, dst, sends, recvs, which, chunk):
+    def send(src, dst, sends, recvs, which, chunk, low=1, high=groups):
         def one(i, carry):
             remote(src, dst, sends, recvs, chunk, i).start()
             return carry
 
-        lax.fori_loop(1, groups, one, 0)
-        own(src, dst, which, chunk).start()
+        lax.fori_loop(low, high, one, 0)
+        if high == groups:
+            own(src, dst, which, chunk).start()
 
     def sent(src, dst, sends, recvs, chunk):
         def one(i, carry):
@@ -177,8 +193,6 @@
     a_way = (sa, ra, sas, ras)
     b_way = (sb, rb, sbs, rbs)
     c_way = (sc, rc, scs, rcs)
-
-    loads[0].wait()
 
     def out_rows(pair, place):
         def one(step, carry):
@@ -199,6 +213,7 @@
         lax.fori_loop(0, 6, one, 0)
 
     def forward_pair(pair, carry):
+        loaded(pair).wait()
         for second in range(2):
             row = 2 * pair + second
             field = vmem[row].astype(F32)
@@ -220,14 +235,14 @@
 
         @pl.when(pair == 0)
         def _():
-            pl.semaphore_wait(barrier, groups - 1 + team - 1)
+            pl.semaphore_wait(barrier, greeted)
 
         send(*a_way, 0, pair)
         return carry
 
     lax.fori_loop(0, pairs, forward_pair, 0)
 
-    loads[1].wait()
+    loads[0].wait()
 
     def cot_pair(pair, carry):
         for second in range(2):
@@ -243,8 +258,8 @@
 
     lax.fori_loop(0, pairs, cot_pair, 0)
 
+    loads[1].wait()
     loads[2].wait()
-    loads[3].wait()
     for which, held in ((0, wa), (1, wb)):
         held[...] = jnp.zeros_like(held)
         real, imag = split(wraw[which, 0]), split(wraw[which, 1])
@@ -372,30 +387,37 @@
         part[384 + 2 * i : 385 + 2 * i, :] = sums[2, row : row + 1, 0:128]
         part[385 + 2 * i : 386 + 2 * i, :] = sums[2, row : row + 1, 128:256]
 
-    share = part.shape[0] // team
+    share = part.shape[0] // plane
 
     def rows_of(at):
         return pl.ds(pl.multiple_of(at * share, share), share)
 
     def scatter(i):
-        to = lax.rem(member + i, team)
         return pltpu.make_async_remote_copy(
-            src_ref=part.at[rows_of(to)],
+            src_ref=part.at[rows_of(lax.rem(flat + i, plane))],
             dst_ref=parts.at[rows_of(i)],
             send_sem=ps.at[i],
             recv_sem=pr.at[i],
-            device_id={"dp": to},
+            device_id={"dp": mate(i)},
             device_id_type=MESH,
         )
 
+    across = pltpu.make_async_remote_copy(
+        src_ref=total.at[0],
+        dst_ref=total.at[1],
+        send_sem=zs,
+        recv_sem=zr,
+        device_id={"dp": twin},
+        device_id_type=MESH,
+    )
+
     def gather(i):
-        to = lax.rem(member + i, team)
         return pltpu.make_async_remote_copy(
-            src_ref=total,
-            dst_ref=done.at[rows_of(member)],
+            src_ref=total.at[2],
+            dst_ref=done.at[rows_of(flat)],
             send_sem=ts.at[i],
             recv_sem=tr.at[i],
-            device_id={"dp": to},
+            device_id={"dp": mate(i)},
             device_id_type=MESH,
         )
 
@@ -404,19 +426,23 @@
             function(i)
             return carry
 
-        lax.fori_loop(1, team, one, 0)
+        lax.fori_loop(1, plane, one, 0)
 
     each(lambda i: scatter(i).start())
-    send(*c_way, 2, 1)
+    send(*c_way, 2, 1, 1, groups // 2)
 
     def add(i, value):
         scatter(i).wait_recv()
         return value + parts[rows_of(i), :]
 
-    total[...] = lax.fori_loop(1, team, add, part[rows_of(member), :]) * norm
+    total[0] = lax.fori_loop(1, plane, add, part[rows_of(flat), :])
+    across.start()
+    send(*c_way, 2, 1, groups // 2, groups)
+    across.wait()
+    total[2] = (total[0] + total[1]) * norm
     each(lambda i: gather(i).start())
     send(*c_way, 2, 2)
-    done[rows_of(member), :] = total[...]
+    done[rows_of(flat), :] = total[2]
 
     def stored(pair):
         return pltpu.make_async_copy(
@@ -471,17 +497,28 @@
     summed.wait()
 
 
-def handover(mixed, grads, out, gw1, gb1, gw2, gb2, held, insem, outsem):
+def handover(
+    mixed, grads, out, gw1, gb1, gw2, gb2,
+    held, summed, weights, biases, insem, outsem, gradsem, sumsem,
+):
     rows = held.shape[0]
     loads = [pltpu.make_async_copy(mixed.at[0, i], held.at[i], insem.at[i]) for i in range(rows)]
     stores = [pltpu.make_async_copy(held.at[i], out.at[0, i], outsem.at[i]) for i in range(rows)]
+    fetch = pltpu.make_async_copy(grads, summed, gradsem)
+    fetch.start()
     for load in loads:
         load.start()
-    for which, ref in ((0, gw1), (1, gw2)):
-        ref[0, 0] = grads[192 * which : 192 * which + 96, 0:BS]
-        ref[0, 1] = grads[192 * which + 96 : 192 * which + 192, 0:BS]
-    gb1[0] = grads[384:386, 0:BS]
-    gb2[0] = grads[386:388, 0:BS]
+    fetch.wait()
+    for which in range(2):
+        for i in range(2):
+            at = 192 * which + 96 * i
+            weights[which, i] = summed[at : at + 96, 0:BS]
+        biases[which] = summed[384 + 2 * which : 386 + 2 * which, 0:BS]
+    for i, (held_in, ref) in enumerate(
+        ((weights.at[0], gw1), (weights.at[1], gw2), (biases.at[0], gb1), (biases.at[1], gb2))
+    ):
+        stores.append(pltpu.make_async_copy(held_in, ref.at[0], sumsem.at[i]))
+        stores[-1].start()
     for load, store in zip(loads, stores):
         load.wait()
         store.start()
@@ -497,9 +534,10 @@
         norm = 1.0 / math.sqrt(team * members.shape[0] * rows * groups * KW)
         made = tables(width, rows * groups, groups)
         moved = pltpu.VMEM((3 * groups * 144, LANES), F32)
-        share = -(-400 // (team * 8)) * 8
+        plane = team // 2
+        share = -(-392 // (plane * 8)) * 8
         sems = pltpu.SemaphoreType.DMA((3, groups))
-        team_sems = pltpu.SemaphoreType.DMA((team,))
+        team_sems = pltpu.SemaphoreType.DMA((plane,))
         modes = KW * rows * groups
         whole = pl.BlockSpec(memory_space=pltpu.VMEM)
         away = pl.BlockSpec(memory_space=pl.ANY)
@@ -507,7 +545,7 @@
             functools.partial(kernel, groups, team, norm),
             out_shape=(
                 jax.ShapeDtypeStruct(members.shape, BF16),
-                jax.ShapeDtypeStruct((share * team, LANES), F32),
+                jax.ShapeDtypeStruct((share * plane, LANES), F32),
             ),
             in_specs=[away, away, whole, away, whole, away, whole] + [whole] * 5,
             out_specs=(away, away),
@@ -525,16 +563,16 @@
                 pltpu.VMEM((3, 256, 256), F32),
                 pltpu.VMEM((8, 256), F32),
                 moved, moved, moved, moved, moved, moved,
-                pltpu.VMEM((share * team, LANES), F32),
-                pltpu.VMEM((share * team, LANES), F32),
-                pltpu.VMEM((share, LANES), F32),
-                pltpu.VMEM((share * team, LANES), F32),
-                pltpu.SemaphoreType.DMA((4,)),
+                pltpu.VMEM((share * plane, LANES), F32),
+                pltpu.VMEM((share * plane, LANES), F32),
+                pltpu.VMEM((3, share, LANES), F32),
+                pltpu.VMEM((share * plane, LANES), F32),
+                pltpu.SemaphoreType.DMA((6,)),
                 pltpu.SemaphoreType.DMA((3,)),
                 pltpu.SemaphoreType.DMA,
                 pltpu.SemaphoreType.DMA((3, 3)),
                 sems, sems, sems, sems, sems, sems,
-                team_sems, team_sems, team_sems, team_sems,
+                team_sems, team_sems, pltpu.SemaphoreType.DMA, pltpu.SemaphoreType.DMA, team_sems, team_sems,
             ],
             compiler_params=pltpu.CompilerParams(
                 collective_id=0, has_side_effects=True, vmem_limit_bytes=56 << 20
@@ -553,12 +591,17 @@
                 jax.ShapeDtypeStruct((1,) + weight_two.shape[1:], F32),
                 jax.ShapeDtypeStruct((1,) + bias_two.shape[1:], F32),
             ),
-            in_specs=[away, whole],
-            out_specs=(away, whole, whole, whole, whole),
+            in_specs=[away, away],
+            out_specs=(away,) * 5,
             scratch_shapes=[
                 pltpu.VMEM((rows, width, channels), BF16),
+                pltpu.VMEM((share * plane, LANES), F32),
+                pltpu.VMEM((2, 2, BS, BS), F32),
+                pltpu.VMEM((2, 2, BS), F32),
                 pltpu.SemaphoreType.DMA((rows,)),
                 pltpu.SemaphoreType.DMA((rows,)),
+                pltpu.SemaphoreType.DMA,
+                pltpu.SemaphoreType.DMA((4,)),
             ],
             name="handover",
         )(mixed, grads)

time: 143 us -> 138 us (0.965)
  the two profiles are of different devices: /device:TPU:32 before, /device:TPU:1 now
where the time goes in v4:
time: 138 us
  Pallas kernels  137 us (99%)
    pallas_call x1, Pallas kernels, shards(): pl.pallas_call(functools.partial(kernel, groups, team, norm), out_shape=(...  135 us

profile of v4, /device:TPU:1, one launch (start us, length us, event | category | flops | bytes accessed | tf_op | source)
XLA Modules:
  0.0 137.8 jit_solution(8942284124464767405)
XLA Ops:
  0.6 134.7 %afno_block.1 = (bf16[1,6,100,768]{3,2,1,0:T(8,128)(2,1)}, f32[512,128]{1,0:T(8,128)}) custom-call(bf16[1,6,100,768]{3,2,1,0:T(8,128)(2,1)} %mem.1, bf16[1,6,100,768]{3,2,1,0:T(8,128)(2,1)} %cot.1, f32[768]{0:T(1024)} %gain.1, f32[8,2,96,96]{3,2,1,0:T(8,128)} %w1.1, f32[8,2,96]{2,1,0:T(2,128)} %b1.1, f32[8,2,96,96]{3,2,1,0:T(8,128)} %w2.1, f32[8,2,96]{2,1,0:T(2,128)} %b2.1, ...), custom_call_target="tpu_custom_call" | custom-call | tf_op jit(solution)/shard_map/afno_block/pallas_call | solution.py:544
  135.3 2.5 %handover.1 = (bf16[1,6,100,768]{3,2,1,0:T(8,128)(2,1)}, f32[1,2,96,96]{3,2,1,0:T(8,128)}, f32[1,2,96]{2,1,0:T(2,128)}, f32[1,2,96,96]{3,2,1,0:T(8,128)}, f32[1,2,96]{2,1,0:T(2,128)}) custom-call(bf16[1,6,100,768]{3,2,1,0:T(8,128)(2,1)} %get-tuple-element.7.mixed, f32[512,128]{1,0:T(8,128)} %get-tuple-element.8.grads), custom_call_target="tpu_custom_call" | custom-call | tf_op jit(solution)/shard_map/handover/pallas_call | solution.py:585

commit v5 on v4

--- a/solution.py
+++ b/solution.py
@@ -97,9 +97,9 @@
 
 def kernel(
     groups, team, norm,
-    mem, cot, gain, w1, b1, w2, b2, lonf, lonc, latf, lati, loni,
+    mem, cot, gain_in, w1, b1_in, w2, b2_in, lonf_in, lonc_in, latf_in, lati_in, loni_in,
     mixed, grads,
-    vmem, vcot, base, lon, wraw, wa, wb, spec, first, mask, sums, biases,
+    gain, b1, b2, lonf, lonc, latf, lati, loni, vmem, vcot, base, lon, wraw, wa, wb, spec, first, mask, sums, biases,
     sa, ra, sb, rb, sc, rc, part, parts, total, done,
     insem, outsem, donesem, locsem, sas, ras, sbs, rbs, scs, rcs, ps, pr, zs, zr, ts, tr,
 ):
@@ -113,14 +113,16 @@
         two = pl.ds(2 * pair, 2)
         return pltpu.make_async_copy(mem.at[0, two], vmem.at[two], insem.at[pair])
 
+    copies = (
+        (lonf_in, lonf), (gain_in, gain), (cot.at[0], vcot), (lonc_in, lonc),
+        (w1.at[me], wraw.at[0]), (w2.at[me], wraw.at[1]), (b1_in, b1), (b2_in, b2),
+        (latf_in, latf), (lati_in, lati), (loni_in, loni),
+    )
     loads = [
-        pltpu.make_async_copy(cot.at[0], vcot, insem.at[3]),
-        pltpu.make_async_copy(w1.at[me], wraw.at[0], insem.at[4]),
-        pltpu.make_async_copy(w2.at[me], wraw.at[1], insem.at[5]),
+        pltpu.make_async_copy(src, dst, insem.at[pairs + i]) for i, (src, dst) in enumerate(copies)
     ]
-    for pair in range(pairs):
-        loaded(pair).start()
-    for load in loads:
+    loaded(0).start()
+    for load in loads[:2]:
         load.start()
 
     barrier = pltpu.get_barrier_semaphore()
@@ -147,11 +149,18 @@
     greet("dp", lambda i: twin, 2)
     greeted = groups - 1 + plane - 1 + 1
 
+    for pair in range(1, pairs):
+        loaded(pair).start()
+    for load in loads[2:]:
+        load.start()
+    for load in loads[:2]:
+        load.wait()
+
     def block(chunk, at):
         return pl.ds(pl.multiple_of((chunk * groups + at) * 144, 144), 144)
 
     def remote(src, dst, send, recv, chunk, i):
-        to = lax.rem(me + i, groups)
+        to = lax.rem(me + groups - i, groups)
         return pltpu.make_async_remote_copy(
             src_ref=src.at[block(chunk, to)],
             dst_ref=dst.at[block(chunk, me)],
@@ -242,7 +251,8 @@
 
     lax.fori_loop(0, pairs, forward_pair, 0)
 
-    loads[0].wait()
+    for load in loads[2:4]:
+        load.wait()
 
     def cot_pair(pair, carry):
         for second in range(2):
@@ -258,8 +268,8 @@
 
     lax.fori_loop(0, pairs, cot_pair, 0)
 
-    loads[1].wait()
-    loads[2].wait()
+    for load in loads[4:]:
+        load.wait()
     for which, held in ((0, wa), (1, wb)):
         held[...] = jnp.zeros_like(held)
         real, imag = split(wraw[which, 0]), split(wraw[which, 1])
@@ -539,7 +549,6 @@
         sems = pltpu.SemaphoreType.DMA((3, groups))
         team_sems = pltpu.SemaphoreType.DMA((plane,))
         modes = KW * rows * groups
-        whole = pl.BlockSpec(memory_space=pltpu.VMEM)
         away = pl.BlockSpec(memory_space=pl.ANY)
         mixed, grads = pl.pallas_call(
             functools.partial(kernel, groups, team, norm),
@@ -547,9 +556,13 @@
                 jax.ShapeDtypeStruct(members.shape, BF16),
                 jax.ShapeDtypeStruct((share * plane, LANES), F32),
             ),
-            in_specs=[away, away, whole, away, whole, away, whole] + [whole] * 5,
+            in_specs=[away] * (7 + len(made)),
             out_specs=(away, away),
             scratch_shapes=[
+                pltpu.VMEM(gain.shape, F32),
+                pltpu.VMEM(bias_one.shape, F32),
+                pltpu.VMEM(bias_two.shape, F32),
+                *[pltpu.VMEM(table.shape, BF16) for table in made],
                 pltpu.VMEM((rows, width, channels), BF16),
                 pltpu.VMEM((rows, width, channels), BF16),
                 pltpu.VMEM((rows, width, channels), F32),
@@ -567,7 +580,7 @@
                 pltpu.VMEM((share * plane, LANES), F32),
                 pltpu.VMEM((3, share, LANES), F32),
                 pltpu.VMEM((share * plane, LANES), F32),
-                pltpu.SemaphoreType.DMA((6,)),
+                pltpu.SemaphoreType.DMA((14,)),
                 pltpu.SemaphoreType.DMA((3,)),
                 pltpu.SemaphoreType.DMA,
                 pltpu.SemaphoreType.DMA((3, 3)),

time: 138 us -> 135 us (0.978)
  the two profiles are of different devices: /device:TPU:1 before, /device:TPU:32 now
where the time goes in v5:
time: 135 us
  Pallas kernels  134 us (99%)
    pallas_call x1, Pallas kernels, shards(): pl.pallas_call(functools.partial(kernel, groups, team, norm), out_shape=(...  132 us

profile of v5, /device:TPU:32, one launch (start us, length us, event | category | flops | bytes accessed | tf_op | source)
XLA Modules:
  0.0 134.9 jit_solution(13569746614291699481)
XLA Ops:
  0.6 131.7 %afno_block.1 = (bf16[1,6,100,768]{3,2,1,0:T(8,128)(2,1)}, f32[512,128]{1,0:T(8,128)}) custom-call(bf16[1,6,100,768]{3,2,1,0:T(8,128)(2,1)} %mem.1, bf16[1,6,100,768]{3,2,1,0:T(8,128)(2,1)} %cot.1, f32[768]{0:T(1024)} %gain_in.1, f32[8,2,96,96]{3,2,1,0:T(8,128)} %w1.1, f32[8,2,96]{2,1,0:T(2,128)} %b1_in.1, f32[8,2,96,96]{3,2,1,0:T(8,128)} %w2.1, ...), custom_call_target="tpu_custom_call" | custom-call | tf_op jit(solution)/shard_map/afno_block/pallas_call | solution.py:553
  132.4 2.5 %handover.1 = (bf16[1,6,100,768]{3,2,1,0:T(8,128)(2,1)}, f32[1,2,96,96]{3,2,1,0:T(8,128)}, f32[1,2,96]{2,1,0:T(2,128)}, f32[1,2,96,96]{3,2,1,0:T(8,128)}, f32[1,2,96]{2,1,0:T(2,128)}) custom-call(bf16[1,6,100,768]{3,2,1,0:T(8,128)(2,1)} %get-tuple-element.7.mixed, f32[512,128]{1,0:T(8,128)} %get-tuple-element.8.grads), custom_call_target="tpu_custom_call" | custom-call | tf_op jit(solution)/shard_map/handover/pallas_call | solution.py:598

commit v6 on v5

--- a/solution.py
+++ b/solution.py
@@ -219,7 +219,7 @@
                         place(step, 4 * group + b, v, three[v])
             return carry
 
-        lax.fori_loop(0, 6, one, 0)
+        lax.fori_loop(0, 6, one, 0, unroll=2)
 
     def forward_pair(pair, carry):
         loaded(pair).wait()
@@ -454,10 +454,8 @@
     send(*c_way, 2, 2)
     done[rows_of(flat), :] = total[2]
 
-    def stored(pair):
-        return pltpu.make_async_copy(
-            vmem.at[pl.ds(2 * pair, 2)], mixed.at[0, pl.ds(2 * pair, 2)], outsem.at[pair]
-        )
+    def stored(row):
+        return pltpu.make_async_copy(vmem.at[row], mixed.at[0, row], outsem.at[row])
 
     summed = pltpu.make_async_copy(done, grads, donesem)
 
@@ -489,19 +487,20 @@
                         )
             return carry
 
-        lax.fori_loop(0, 6, one, 0)
+        lax.fori_loop(0, 6, one, 0, unroll=2)
         for second in range(2):
             row = 2 * pair + second
             spectral = dot(loni[...], lon[second].astype(BF16))
             vmem[row] = (base[row] + spectral).astype(BF16)
-        stored(pair).start()
+            stored(row).start()
         if pair == 1:
             each(lambda i: gather(i).wait_recv())
             summed.start()
 
     for pair in range(pairs):
         sent(*c_way, pair)
-        stored(pair).wait()
+    for row in range(2 * pairs):
+        stored(row).wait()
     each(lambda i: scatter(i).wait_send())
     each(lambda i: gather(i).wait_send())
     summed.wait()
@@ -543,7 +542,7 @@
         _, rows, width, channels = members.shape
         norm = 1.0 / math.sqrt(team * members.shape[0] * rows * groups * KW)
         made = tables(width, rows * groups, groups)
-        moved = pltpu.VMEM((3 * groups * 144, LANES), F32)
+        moved = pltpu.VMEM((3 * groups * 144 + 144, LANES), F32)
         plane = team // 2
         share = -(-392 // (plane * 8)) * 8
         sems = pltpu.SemaphoreType.DMA((3, groups))
@@ -581,7 +580,7 @@
                 pltpu.VMEM((3, share, LANES), F32),
                 pltpu.VMEM((share * plane, LANES), F32),
                 pltpu.SemaphoreType.DMA((14,)),
-                pltpu.SemaphoreType.DMA((3,)),
+                pltpu.SemaphoreType.DMA((rows,)),
                 pltpu.SemaphoreType.DMA,
                 pltpu.SemaphoreType.DMA((3, 3)),
                 sems, sems, sems, sems, sems, sems,

time: 135 us -> 135 us (level)
  no operation moved by 1% of the time
where the time goes in v6:
time: 135 us; the launch traced here: 134 us
  Pallas kernels  134 us (99%)
    pallas_call x1, Pallas kernels, shards(): pl.pallas_call(functools.partial(kernel, groups, team, norm), out_shape=(...  131 us

profile of v6, /device:TPU:32, one launch (start us, length us, event | category | flops | bytes accessed | tf_op | source)
XLA Modules:
  0.0 134.5 jit_solution(13410879311454940633)
XLA Ops:
  0.6 131.4 %afno_block.1 = (bf16[1,6,100,768]{3,2,1,0:T(8,128)(2,1)}, f32[512,128]{1,0:T(8,128)}) custom-call(bf16[1,6,100,768]{3,2,1,0:T(8,128)(2,1)} %mem.1, bf16[1,6,100,768]{3,2,1,0:T(8,128)(2,1)} %cot.1, f32[768]{0:T(1024)} %gain_in.1, f32[8,2,96,96]{3,2,1,0:T(8,128)} %w1.1, f32[8,2,96]{2,1,0:T(2,128)} %b1_in.1, f32[8,2,96,96]{3,2,1,0:T(8,128)} %w2.1, ...), custom_call_target="tpu_custom_call" | custom-call | tf_op jit(solution)/shard_map/afno_block/pallas_call | solution.py:552
  132.0 2.5 %handover.1 = (bf16[1,6,100,768]{3,2,1,0:T(8,128)(2,1)}, f32[1,2,96,96]{3,2,1,0:T(8,128)}, f32[1,2,96]{2,1,0:T(2,128)}, f32[1,2,96,96]{3,2,1,0:T(8,128)}, f32[1,2,96]{2,1,0:T(2,128)}) custom-call(bf16[1,6,100,768]{3,2,1,0:T(8,128)(2,1)} %get-tuple-element.7.mixed, f32[512,128]{1,0:T(8,128)} %get-tuple-element.8.grads), custom_call_target="tpu_custom_call" | custom-call | tf_op jit(solution)/shard_map/handover/pallas_call | solution.py:597

commit v7 on v6

--- a/solution.py
+++ b/solution.py
@@ -219,7 +219,7 @@
                         place(step, 4 * group + b, v, three[v])
             return carry
 
-        lax.fori_loop(0, 6, one, 0, unroll=2)
+        lax.fori_loop(0, 6, one, 0, unroll=3)
 
     def forward_pair(pair, carry):
         loaded(pair).wait()
@@ -487,7 +487,7 @@
                         )
             return carry
 
-        lax.fori_loop(0, 6, one, 0, unroll=2)
+        lax.fori_loop(0, 6, one, 0, unroll=3)
         for second in range(2):
             row = 2 * pair + second
             spectral = dot(loni[...], lon[second].astype(BF16))

time: 135 us -> 135 us (level)
  no operation moved by 1% of the time
where the time goes in v7:
time: 135 us; the launch traced here: 134 us
  Pallas kernels  134 us (99%)
    pallas_call x1, Pallas kernels, shards(): pl.pallas_call(functools.partial(kernel, groups, team, norm), out_shape=(...  131 us

profile of v7, /device:TPU:32, one launch (start us, length us, event | category | flops | bytes accessed | tf_op | source)
XLA Modules:
  0.0 134.5 jit_solution(11714659355938710372)
XLA Ops:
  0.6 131.3 %afno_block.1 = (bf16[1,6,100,768]{3,2,1,0:T(8,128)(2,1)}, f32[512,128]{1,0:T(8,128)}) custom-call(bf16[1,6,100,768]{3,2,1,0:T(8,128)(2,1)} %mem.1, bf16[1,6,100,768]{3,2,1,0:T(8,128)(2,1)} %cot.1, f32[768]{0:T(1024)} %gain_in.1, f32[8,2,96,96]{3,2,1,0:T(8,128)} %w1.1, f32[8,2,96]{2,1,0:T(2,128)} %b1_in.1, f32[8,2,96,96]{3,2,1,0:T(8,128)} %w2.1, ...), custom_call_target="tpu_custom_call" | custom-call | tf_op jit(solution)/shard_map/afno_block/pallas_call | solution.py:552
  132.0 2.5 %handover.1 = (bf16[1,6,100,768]{3,2,1,0:T(8,128)(2,1)}, f32[1,2,96,96]{3,2,1,0:T(8,128)}, f32[1,2,96]{2,1,0:T(2,128)}, f32[1,2,96,96]{3,2,1,0:T(8,128)}, f32[1,2,96]{2,1,0:T(2,128)}) custom-call(bf16[1,6,100,768]{3,2,1,0:T(8,128)(2,1)} %get-tuple-element.7.mixed, f32[512,128]{1,0:T(8,128)} %get-tuple-element.8.grads), custom_call_target="tpu_custom_call" | custom-call | tf_op jit(solution)/shard_map/handover/pallas_call | solution.py:597
